TPU v7x, 32 devices: a whole 2x2x4 slice. The times are simulated.
32 devices in a mesh: lat: 4 (over y, core), lon: 8 (over z, x).
Axes of the slice: x: 2, y: 2, z: 4, core: 2. Of those that a mesh axis runs over, the one named last changes fastest.
Arguments:
- losses: float32 [8, 16, 512, 256], P('lat', 'lon'), may hold values from -6 to 6
- positions: float32 [8, 16, 2, 512], P('lat', 'lon'), may hold values from 0 to 1
- leaf_basis: float32 [8, 16, 512, 64], P('lat', 'lon'), may hold values from -0.25 to 0.25
- near_flags: int32 [8, 16, 9], P('lat', 'lon'), may hold values from 0 to 1, as said below
- leaf_coupling: bfloat16 [8, 16, 36, 64, 64], P('lat', 'lon'), may hold values from -0.75 to 0.75
- leaf_transfer: float32 [8, 16, 64, 64], P('lat', 'lon'), may hold values from -0.75 to 0.75
- device_coupling: bfloat16 [4, 8, 36, 64, 64], P('lat', 'lon'), may hold values from -0.1875 to 0.1875
- device_transfer: float32 [4, 8, 64, 64], replicated, may hold values from -0.75 to 0.75
- group_coupling: bfloat16 [2, 4, 2, 4, 64, 64], replicated, may hold values from -0.09375 to 0.09375
Outputs:
- applied: float32 [8, 16, 512, 256], P('lat', 'lon')
Inputs may be any that keep to these rules, and one draw needn't show every extreme that they name: near_flags[i, j, 3 (di + 1) + dj + 1] is 1 when leaf (i + di, (j + dj) mod 16) forms a dense block with leaf (i, j); the flags of a pair agree seen from both leaves, the middle flag is always 1, and flags toward latitude indices outside the grid are 0.
All inputs are finite; a program needn't handle non-finite values.
Results may differ from a plain program's by a relative error of at most 0.0003.
Values sent between devices are 32-bit elements; how exact they have to be, the bound alone decides.
No kernel may reach another device: no remote copies, remote signals or barrier semaphores. Data moves between devices by JAX's collectives and lax.ppermute only.
A program may use at most 192 MiB of HBM per device.

v0:
```python
import functools

import jax
import jax.numpy as jnp
from jax import lax
from jax.experimental import pallas as pl
from jax.experimental.pallas import tpu as pltpu
from jax.sharding import PartitionSpec as P

PTS = 512
RANK = 64
COLS = 256
HALF = 256
QUAD = 4 * RANK
MSG = QUAD + 16

LN2 = 0.6931471805599453
UNIT = 1.7320508075688772 / 0.15 / LN2

f32 = jnp.float32
bf16 = jnp.bfloat16
VMEM = pltpu.VMEM
SMEM = pltpu.SMEM
whole = pl.BlockSpec(memory_space=VMEM)
scalars = pl.BlockSpec(memory_space=SMEM)


def split(x):
    hi = x.astype(bf16)
    return hi, (x - hi.astype(f32)).astype(bf16)


def mm(a, b, dims=(1, 0)):
    return lax.dot_general(
        a, b, (((dims[0],), (dims[1],)), ((), ())), preferred_element_type=f32
    )


def mm3(a, b, dims=(1, 0)):
    a_hi, a_lo = split(a)
    b_hi, b_lo = split(b)
    return mm(a_hi, b_hi, dims) + (mm(a_lo, b_hi, dims) + mm(a_hi, b_lo, dims))


def mm2(a, b):
    b_hi, b_lo = split(b)
    return mm(a, b_hi) + mm(a, b_lo)


def params(limit=64):
    return pltpu.CompilerParams(vmem_limit_bytes=limit * 1024 * 1024)


COST = pl.CostEstimate(flops=20_000_000_000, bytes_accessed=4_000_000, transcendentals=0)
LOW = pl.CostEstimate(flops=1_000, bytes_accessed=1_000, transcendentals=0)


def shape(*dims):
    return jax.ShapeDtypeStruct(dims, f32)


def lat_parity():
    return lax.rem(lax.axis_index("lat"), 2)


def coef_kernel(
    loss, basis, transfer, pos, a_right, a_left, b_right, b_left, to_y, to_c, place8, dev,
    values, bases, message, sems, load_sems,
):
    parity = lat_parity()
    loads = [
        (
            pltpu.make_async_copy(loss.at[leaf], values.at[leaf], load_sems.at[leaf]),
            pltpu.make_async_copy(basis.at[leaf], bases.at[leaf], load_sems.at[4 + leaf]),
        )
        for leaf in range(4)
    ]
    for pair in loads:
        for copy in pair:
            copy.start()
    for leaf in range(4):
        place = pos[leaf] * UNIT
        place8[leaf] = jnp.concatenate([place, jnp.zeros((6, PTS), f32)], 0)
        for coord in range(2):
            for half in range(2):
                at = QUAD + 4 * leaf + 2 * coord + half
                message[at : at + 1, :] = place[coord : coord + 1, half * HALF : (half + 1) * HALF]
    for pair in loads:
        for copy in pair:
            copy.wait()
    y_row, c_row = 2 * parity, 2 - 2 * parity
    first, second = slice(0, PTS), slice(PTS, 2 * PTS)
    copies = []
    for source, target in (
        (y_row + 1, a_right.at[first]),
        (y_row, a_left.at[first]),
        (c_row + 1, b_right),
        (c_row, b_left),
        (y_row, to_y.at[first]),
        (y_row + 1, to_y.at[second]),
        (c_row, to_c.at[first]),
        (c_row + 1, to_c.at[second]),
    ):
        copy = pltpu.make_async_copy(values.at[source], target, sems.at[len(copies)])
        copy.start()
        copies.append(copy)
    total = None
    for leaf in range(4):
        l_hi, l_lo = split(values[leaf])
        b_hi, b_lo = split(bases[leaf])
        coef = mm(b_hi, l_hi) + (mm(b_lo, l_hi) + mm(b_hi, l_lo))
        message[leaf * RANK : (leaf + 1) * RANK, :] = coef
        part = mm3(transfer[leaf], coef, (0, 0))
        total = part if leaf == 0 else total + part
    dev[...] = total
    for target in (
        a_right.at[PTS:], a_left.at[PTS:], to_y.at[2 * PTS :], to_c.at[2 * PTS :]
    ):
        copy = pltpu.make_async_copy(message, target, sems.at[len(copies)])
        copy.start()
        copies.append(copy)
    for copy in copies:
        copy.wait()


hbm = pl.BlockSpec(memory_space=pl.ANY)


def coefficients(losses, basis, transfer, positions):
    return pl.pallas_call(
        coef_kernel,
        in_specs=[hbm, hbm, whole, whole],
        out_specs=[hbm] * 6 + [whole] * 2,
        out_shape=[
            shape(PTS + MSG, COLS),
            shape(PTS + MSG, COLS),
            shape(PTS, COLS),
            shape(PTS, COLS),
            shape(2 * PTS + MSG, COLS),
            shape(2 * PTS + MSG, COLS),
            shape(4, 8, PTS),
            shape(RANK, COLS),
        ],
        scratch_shapes=[
            VMEM((4, PTS, COLS), f32),
            VMEM((4, RANK, PTS), f32),
            VMEM((MSG, COLS), f32),
            pltpu.SemaphoreType.DMA((12,)),
            pltpu.SemaphoreType.DMA((8,)),
        ],
        compiler_params=params(),
        cost_estimate=COST,
        name="coefs",
    )(losses, basis, transfer, positions)


def near_scratch(n_slots, n_pairs):
    return [
        SMEM((n_pairs + 1, 8), jnp.int32),
        VMEM((4, PTS, 8), f32),
        VMEM((n_slots, 8, PTS), f32),
        VMEM((n_slots, 2 * PTS, COLS), bf16),
        VMEM((PTS, 2 * PTS), bf16),
        VMEM((PTS, 2 * PTS), bf16),
        VMEM((4, PTS, COLS), f32),
        VMEM((n_slots, PTS, COLS), f32),
        VMEM((n_slots, 16, COLS), f32),
        pltpu.SemaphoreType.DMA((8 + 2 * n_slots,)),
    ]


def near_blocks(flags, place8, slots, pairs, before, out, scratch, fill=None):
    table, tpos, spos, stack, kern_a, kern_b, acc, stage, marks, sems = scratch
    arrivals = []
    for slot, (values, places, _) in enumerate(slots):
        pair = (
            pltpu.make_async_copy(values, stage.at[slot], sems.at[8 + 2 * slot]),
            pltpu.make_async_copy(places, marks.at[slot], sems.at[9 + 2 * slot]),
        )
        for copy in pair:
            copy.start()
        arrivals.append(pair)
    loads = []
    if before is not None:
        loads = [
            pltpu.make_async_copy(before.at[leaf], acc.at[leaf], sems.at[leaf])
            for leaf in range(4)
        ]
    for copy in loads:
        copy.start()
    for leaf in range(4):
        tpos[leaf] = place8[leaf].T
    for slot, (_, _, base) in enumerate(slots):
        for copy in arrivals[slot]:
            copy.wait()
        hi, lo = split(stage[slot])
        stack[slot, :PTS, :] = hi
        stack[slot, PTS:, :] = lo
        for coord in range(2):
            for half in range(2):
                spos[slot, coord : coord + 1, half * HALF : (half + 1) * HALF] = marks[
                    slot, pl.ds(base + 2 * coord + half, 1), :
                ]
    count = 0
    for slot, row, col, own_row, own_col in pairs:
        target = 2 * own_row + own_col
        table[count, 0] = slot
        table[count, 1] = target
        table[count, 2] = row - own_row
        table[count, 3] = col - own_col
        flag = flags[target, 3 * (row - own_row + 1) + col - own_col + 1]
        count = count + jnp.where(flag > 0, 1, 0)

    def evaluate(index, half, kern):
        slot, target = table[index, 0], table[index, 1]
        src_row = spos[slot, 0:1, :] + table[index, 2].astype(f32) * UNIT
        src_col = spos[slot, 1:2, :] + table[index, 3].astype(f32) * UNIT
        part = slice(half * HALF, (half + 1) * HALF)
        d_row = tpos[target, part, 0:1] - src_row
        d_col = tpos[target, part, 1:2] - src_col
        square = d_row * d_row + d_col * d_col
        dist = square * lax.rsqrt(jnp.maximum(square, 1e-30))
        decay = jnp.exp2(-dist)
        hi, lo = split(decay + decay * (dist * LN2))
        kern[part, :PTS] = hi
        kern[part, PTS:] = lo

    def apply(index, half, kern):
        slot, target = table[index, 0], table[index, 1]
        part = slice(half * HALF, (half + 1) * HALF)
        l_hi = stack[slot, :PTS, :]
        l_lo = stack[slot, PTS:, :]
        k_hi = kern[part, :PTS]
        k_lo = kern[part, PTS:]
        acc[target, part, :] += mm(k_hi, l_hi) + mm(k_lo, l_hi) + mm(k_hi, l_lo)

    def step(index, kern, other):
        following = jnp.minimum(index + 1, count - 1)
        for half in range(2):
            evaluate(following, half, other)
            apply(index, half, kern)

    @pl.when(count > 0)
    def _():
        for half in range(2):
            evaluate(0, half, kern_a)

    for copy in loads:
        copy.wait()
    if fill is not None:
        fill(acc, stage)

    @pl.loop(0, (count + 1) // 2)
    def _(pair):
        step(2 * pair, kern_a, kern_b)

        @pl.when(2 * pair + 1 < count)
        def _():
            step(2 * pair + 1, kern_b, kern_a)


    stores = [
        pltpu.make_async_copy(acc.at[leaf], out.at[leaf], sems.at[4 + leaf]) for leaf in range(4)
    ]
    for copy in stores:
        copy.start()
    for copy in stores:
        copy.wait()


ACC = shape(4, PTS, COLS)


def block(ref, start, rows):
    return ref.at[pl.ds(start, rows)]


def own_kernel(flags, place8, loss, msg, out, *scratch):
    slots = [(loss.at[leaf], block(msg, PTS + QUAD, 16), 4 * leaf) for leaf in range(4)]
    pairs = [(s, s // 2, s % 2, t // 2, t % 2) for s in range(4) for t in range(4)]

    def fill(acc, losses):
        for leaf in range(4):
            acc[leaf] = 0.5 * losses[leaf]

    near_blocks(flags, place8, slots, pairs, None, out, scratch, fill)


def lat_kernel(flags, place8, from_y, from_c, before, out, *scratch):
    parity = lat_parity()
    slots, pairs = [], []
    for ref, place, row, own_row in (
        (from_y, 8 - 8 * parity, 3 * parity - 1, parity),
        (from_c, 8 * parity, 2 - 3 * parity, 1 - parity),
    ):
        for col in range(2):
            for own_col in range(2):
                pairs.append((len(slots), row, col, own_row, own_col))
            slots.append(
                (block(ref, col * PTS, PTS), block(ref, 2 * PTS + QUAD, 16), place + 4 * col)
            )
    near_blocks(flags, place8, slots, pairs, before, out, scratch)


def lon_kernel(flags, place8, left, right, before, out, *scratch):
    parity = lat_parity()
    at = PTS + QUAD
    slots = [
        (block(left, 0, PTS), block(left, at, 16), 8 * parity + 4),
        (block(right, 0, PTS), block(right, at, 16), 8 * parity),
    ]
    pairs = [(s, parity, 3 * s - 1, i, s) for s in range(2) for i in range(2)]
    near_blocks(flags, place8, slots, pairs, before, out, scratch)


def last_kernel(
    flags, place8, a_left, a_right, left, right, c_ends, left_c, right_c, before, out, *scratch
):
    parity = lat_parity()
    at = PTS + QUAD
    own_place, far_place = 8 - 8 * parity, 8 * parity
    slots = [
        (left, block(a_left, at, 16), own_place + 4),
        (right, block(a_right, at, 16), own_place),
        (left_c, block(c_ends, QUAD, 16), far_place + 4),
        (right_c, block(c_ends, MSG + QUAD, 16), far_place),
    ]
    pairs = [(s, 1 - parity, 3 * s - 1, i, s) for s in range(2) for i in range(2)]
    pairs += [(2 + s, 2 - 3 * parity, 3 * s - 1, 1 - parity, s) for s in range(2)]
    near_blocks(flags, place8, slots, pairs, before, out, scratch)


def near(kernel, name, n_slots, n_pairs, operands, chained=True, cost=None, scratch=()):
    return pl.pallas_call(
        kernel,
        in_specs=[scalars, whole] + [hbm] * (len(operands) - 2),
        out_specs=[hbm],
        out_shape=[ACC],
        scratch_shapes=near_scratch(n_slots, n_pairs) + list(scratch),
        input_output_aliases={len(operands) - 1: 0} if chained else {},
        compiler_params=params(),
        cost_estimate=cost or COST,
        name=name,
    )(*operands)


def window_sum(flags, weights, bands, first=0):
    total = None
    for base, cells in bands:
        for v in range(6):
            if cells[v // 2] is None:
                continue
            ref, offset = cells[v // 2]
            for a in range(2):
                start = offset + (2 * a + v % 2) * RANK
                hi, lo = split(ref[start : start + RANK, :])
                u = base + a
                w = 6 * u + v
                rows = []
                for leaf in range(4):
                    part_w = weights[leaf, w - first]
                    d_row = u - 2 - leaf // 2
                    d_col = v - 2 - leaf % 2
                    if abs(d_col) <= 1:
                        inside = (d_row >= -1) & (d_row <= 1)
                        flag = flags[leaf, 3 * jnp.clip(d_row + 1, 0, 2) + d_col + 1]
                        keep = 1 - jnp.where(inside, flag, 0)
                        part_w = (part_w.astype(f32) * keep.astype(f32)).astype(bf16)
                    rows.append(part_w)
                stacked = jnp.concatenate(rows, 0)
                part = mm(stacked, hi) + mm(stacked, lo)
                total = part if total is None else total + part
    return total


def far_kernel(
    n_lat, n_lon, flags, weights, own, left, right, from_y, from_c, devices, c_ends,
    dev_w, dev_t, group_w, leaf_t, out, weights_v, cells, rows_dev, dev_w_v, dev_t_v,
    group_row_w, leaf_t_v, sems,
):
    lat = lax.axis_index("lat")
    lon = lax.axis_index("lon")
    parity = lax.rem(lat, 2)
    side = lax.rem(lon, 2)
    group_row, group_col = lat // 2, lon // 2
    n_gcol = n_lon // 2
    size = 2 * n_lon * RANK
    copies = []
    for source, target in (
        (dev_w, dev_w_v),
        (block(devices, 2 * MSG, size), rows_dev.at[0]),
        (block(c_ends, 2 * MSG, size), rows_dev.at[1]),
        (group_w.at[group_row, group_col], group_row_w),
        (dev_t, dev_t_v),
        (leaf_t, leaf_t_v),
        (block(own, PTS, QUAD), cells.at[0]),
        (block(left, PTS, QUAD), cells.at[1]),
        (block(right, PTS, QUAD), cells.at[2]),
        (block(from_y, 2 * PTS, QUAD), cells.at[3]),
        (block(from_c, 2 * PTS, QUAD), cells.at[4]),
        (block(c_ends, 0, QUAD), cells.at[5]),
        (block(c_ends, MSG, QUAD), cells.at[6]),
        (weights.at[0], weights_v.at[0]),
        (weights.at[1], weights_v.at[1]),
        (weights.at[2], weights_v.at[2]),
        (weights.at[3], weights_v.at[3]),
    ):
        copy = pltpu.make_async_copy(source, target, sems.at[len(copies)])
        copy.start()
        copies.append(copy)
    for copy in copies[:3]:
        copy.wait()

    def device_coef(k, back, col_side):
        which = jnp.where(side == col_side, 0, 1)
        start = pl.multiple_of((4 * back + 2 * (k // 2) + which) * RANK, RANK)
        return rows_dev[k % 2, pl.ds(start, RANK), :]

    total = jnp.zeros((RANK, COLS), f32)
    for k in range(n_lat):
        other = lat + k - 2 * (lat & k)
        u = other + 2 - 2 * group_row
        for v in range(6):
            shift = 2 * group_col - 2 + v
            drop = (jnp.abs(other - lat) <= 1) & (jnp.abs(shift - lon) <= 1)
            scale = jnp.where(drop, 0.0, 1.0)
            coef = device_coef(k, (1 - v // 2) % n_gcol, v % 2)
            total = total + scale * mm2(dev_w_v[6 * u + v], coef)
    for copy in copies[3:6]:
        copy.wait()

    def group_step(step, field):
        gcol = lax.rem(group_col + step, n_gcol)
        for pair in range(n_lat // 2):
            grow = group_row + pair - 2 * (group_row & pair)
            coef = jnp.zeros((RANK, COLS), f32)
            for e in range(2):
                k = 2 * pair + e
                other = lat + k - 2 * (lat & k)
                for f in range(2):
                    cell = other * n_lon + 2 * gcol + f
                    coef = coef + mm3(dev_t_v[cell], device_coef(k, n_gcol - step, f), (0, 0))
            field = field + mm2(group_row_w[grow, gcol], coef)
        return field

    field = lax.fori_loop(2, n_gcol - 1, group_step, jnp.zeros((RANK, COLS), f32))
    total = total + mm3(dev_t_v[lat * n_lon + lon], field)
    for copy in copies[6:]:
        copy.wait()
    far = window_sum(
        flags,
        weights_v,
        (
            (2, tuple((cells.at[i], 0) for i in (1, 0, 2))),
            (4 * parity, (None, (cells.at[3], 0), None)),
            (4 - 4 * parity, tuple((cells.at[i], 0) for i in (5, 4, 6))),
        ),
    )
    for leaf in range(4):
        rows = slice(leaf * RANK, (leaf + 1) * RANK)
        out[rows, :] = far[rows, :] + mm3(leaf_t_v[leaf], total)


def far_field(n_lat, n_lon, operands):
    return pl.pallas_call(
        functools.partial(far_kernel, n_lat, n_lon),
        in_specs=[scalars] + [hbm] * 12,
        out_specs=whole,
        out_shape=shape(QUAD, COLS),
        scratch_shapes=[
            VMEM((4, 36, RANK, RANK), bf16),
            VMEM((7, QUAD, COLS), f32),
            VMEM((2, 2 * n_lon * RANK, COLS), f32),
            VMEM((36, RANK, RANK), bf16),
            VMEM((n_lat * n_lon, RANK, RANK), f32),
            VMEM((n_lat // 2, n_lon // 2, RANK, RANK), bf16),
            VMEM((4, RANK, RANK), f32),
            pltpu.SemaphoreType.DMA((17,)),
        ],
        compiler_params=params(),
        cost_estimate=LOW,
        name="far",
    )(*operands)


def pack_kernel(*refs):
    parts, (out, sems) = refs[:-2], refs[-2:]
    copies = []
    row = 0
    for index, part in enumerate(parts):
        source = block(part, PTS, MSG) if index < 2 else part
        size = source.shape[0]
        copies.append(pltpu.make_async_copy(source, block(out, row, size), sems.at[index]))
        copies[-1].start()
        row += size
    for copy in copies:
        copy.wait()


def pack(left, right, devices):
    parts = [left, right, *devices]
    rows = 2 * MSG + sum(part.shape[0] for part in devices)
    return pl.pallas_call(
        pack_kernel,
        in_specs=[hbm] * len(parts),
        out_specs=whole,
        out_shape=shape(rows, COLS),
        scratch_shapes=[pltpu.SemaphoreType.DMA((len(parts),))],
        compiler_params=params(),
        cost_estimate=LOW,
        name="pack",
    )(*parts)


def down_kernel(
    flags, place8, weights, left_y, right_y, partial, basis, before, out, *scratch
):
    parity = lat_parity()
    near_refs, (weights_v, cells, basis_v, sems) = scratch[:-4], scratch[-4:]
    at = PTS + QUAD
    copies = []
    for source, target in (
        (block(left_y, PTS, QUAD), cells.at[0]),
        (block(right_y, PTS, QUAD), cells.at[1]),
        (partial, cells.at[2]),
        (weights.at[:, pl.ds(24 * parity, 12)], weights_v),
        (basis, basis_v),
    ):
        copy = pltpu.make_async_copy(source, target, sems.at[len(copies)])
        copy.start()
        copies.append(copy)

    def fill(acc, _):
        for copy in copies:
            copy.wait()
        band = (4 * parity, ((cells.at[0], 0), None, (cells.at[1], 0)))
        far = cells[2] + window_sum(flags, weights_v, (band,), 24 * parity)
        for leaf in range(4):
            acc[leaf] += mm3(basis_v[leaf], far[leaf * RANK : (leaf + 1) * RANK, :], (0, 0))

    base = 8 - 8 * parity
    slots = [
        (block(left_y, 0, PTS), block(left_y, at, 16), base + 4),
        (block(right_y, 0, PTS), block(right_y, at, 16), base),
    ]
    pairs = [(s, 3 * parity - 1, 3 * s - 1, parity, s) for s in range(2)]
    near_blocks(flags, place8, slots, pairs, before, out, near_refs, fill)


def local(
    losses,
    positions,
    leaf_basis,
    near_flags,
    leaf_coupling,
    leaf_transfer,
    device_coupling,
    device_transfer,
    group_coupling,
):
    n_lat = lax.axis_size("lat")
    n_lon = lax.axis_size("lon")

    flat = losses.reshape(4, PTS, COLS)
    basis = jnp.swapaxes(leaf_basis, 2, 3).reshape(4, RANK, PTS)
    flags = near_flags.reshape(4, 9)
    weights = leaf_coupling.reshape(4, 36, RANK, RANK)
    transfer = leaf_transfer.reshape(4, RANK, RANK)

    to_right = [(i, (i + 1) % n_lon) for i in range(n_lon)]
    to_left = [(i, (i - 1) % n_lon) for i in range(n_lon)]
    in_chip = [(i, i ^ 1) for i in range(n_lat)]
    across = [(i, i + 1 if i % 2 else i - 1) for i in range(n_lat)]
    across = [(a, b) for a, b in across if 0 <= b < n_lat]

    across_two = [(i, i ^ 2) for i in range(n_lat)]
    partner = [(i, i ^ 1) for i in range(n_lon)]
    barrier = lax.optimization_barrier

    a_right, a_left, b_right, b_left, to_y, to_c, place8, dev = coefficients(
        flat, basis, transfer, positions.reshape(4, 2, PTS)
    )
    dev_pair = lax.ppermute(dev, "lon", partner)
    from_c = lax.ppermute(to_c, "lat", in_chip)
    dev_pair, to_y = barrier((dev_pair, to_y))
    from_y = lax.ppermute(to_y, "lat", across)

    left = lax.ppermute(a_right, "lon", to_right)
    right = lax.ppermute(a_left, "lon", to_left)
    pair = jnp.concatenate([dev, dev_pair], 0)
    pair_two = lax.ppermute(pair, "lat", across_two)
    quad = jnp.concatenate([pair, pair_two], 0)

    def rotate(step):
        return lax.ppermute(quad, "lon", [(i, (i + step) % n_lon) for i in range(n_lon)])

    first, last = rotate(2), rotate(n_lon - 2)
    from_c, quad, place8 = barrier((from_c, quad, place8))
    (acc,) = near(own_kernel, "own", 4, 16, (flags, place8, flat, a_right), chained=False)
    from_y, first, last, quad, acc = barrier((from_y, first, last, quad, acc))
    moved = [first, *(rotate(step) for step in range(4, n_lon - 2, 2)), last]
    (acc,) = near(lat_kernel, "lat", 4, 8, (flags, place8, from_y, from_c, acc))
    left, right, b_right, b_left, acc = barrier((left, right, b_right, b_left, acc))
    left_b = lax.ppermute(b_right, "lon", to_right)
    right_b = lax.ppermute(b_left, "lon", to_left)
    left_y = lax.ppermute(left, "lat", across)
    right_y = lax.ppermute(right, "lat", across)
    to_c = pack(left, right, (quad, *moved))
    c_ends = lax.ppermute(to_c, "lat", in_chip)
    (acc,) = near(lon_kernel, "lon", 2, 4, (flags, place8, left, right, acc))
    c_ends, acc = barrier((c_ends, acc))
    partial = far_field(
        n_lat,
        n_lon,
        (
            flags,
            weights,
            a_right,
            left,
            right,
            from_y,
            from_c,
            to_c,
            c_ends,
            device_coupling.reshape(36, RANK, RANK),
            device_transfer.reshape(n_lat * n_lon, RANK, RANK),
            group_coupling,
            transfer,
        ),
    )
    left_y, right_y, partial = barrier((left_y, right_y, partial))
    (acc,) = near(
        down_kernel,
        "down",
        2,
        2,
        (flags, place8, weights, left_y, right_y, partial, basis, acc),
        cost=LOW,
        scratch=[
            VMEM((4, 12, RANK, RANK), bf16),
            VMEM((3, QUAD, COLS), f32),
            VMEM((4, RANK, PTS), f32),
            pltpu.SemaphoreType.DMA((5,)),
        ],
    )
    left_b, right_b, acc = barrier((left_b, right_b, acc))
    left_c = lax.ppermute(left_b, "lat", in_chip)
    right_c = lax.ppermute(right_b, "lat", in_chip)
    (acc,) = near(
        last_kernel,
        "last",
        4,
        6,
        (flags, place8, left, right, left_b, right_b, c_ends, left_c, right_c, acc),
    )
    return acc.reshape(2, 2, PTS, COLS)


def solution(mesh):
    placed = (
        P("lat", "lon", None, None),
        P("lat", "lon", None, None),
        P("lat", "lon", None, None),
        P("lat", "lon", None),
        P("lat", "lon", None, None, None),
        P("lat", "lon", None, None),
        P("lat", "lon", None, None, None),
        P(),
        P(),
    )
    return jax.shard_map(
        local, mesh=mesh, in_specs=placed, out_specs=P("lat", "lon", None, None), check_vma=False
    )
```

profile of v0, /device:TPU:0, one launch (start us, length us, event | category | flops | bytes accessed | tf_op | source)
XLA Modules:
  0.0 98.3 jit_solution(546070430423003525)
XLA Ops:
  0.0 5.7 %coefs.1 = (f32[784,256]{1,0:T(8,128)}, f32[784,256]{1,0:T(8,128)}, f32[512,256]{1,0:T(8,128)}, f32[512,256]{1,0:T(8,128)}, f32[1296,256]{1,0:T(8,128)}, /*index...) custom-call(f32[4,512,256]{2,1,0:T(8,128)} %bitcast.25, f32[4,64,512]{2,1,0:T(8,128)} %bitcast.15, ...), custom_call_target="tpu_custom_call" | custom-call | flops 20000000000 | bytes 4000000 | tf_op jit(solution)/shard_map/coefs/pallas_call | solution.py:130
  5.8 0.5 collective-permute-start
  6.3 2.6 %collective-permute-start.1 = (f32[64,256]{1,0:T(8,128)}, f32[64,256]{1,0:T(8,128)S(1)}, u32[]{:S(2)}, u32[]{:S(2)}) collective-permute-start(f32[64,256]{1,0:T(8,128)} %get-tuple-element.37), channel_id=1, source_target_pairs={{0,1},{1,0},{2,3},{3,2},{4,5},{5,4},{6,7},{7,6},{8,9},{9,8},{10,11... | collective-permute-start | bytes 196616 | tf_op jit(solution)/shard_map/ppermute | solution.py:583
  8.8 0.1 collective-permute-start.3
  8.9 4.6 %collective-permute-start.4 = (f32[784,256]{1,0:T(8,128)}, f32[784,256]{1,0:T(8,128)}, u32[]{:S(2)}, u32[]{:S(2)}) collective-permute-start(f32[784,256]{1,0:T(8,128)} %get-tuple-element.43), channel_id=1, source_target_pairs={{0,7},{1,0},{2,1},{3,2},{4,3},{5,4},{6,5},{7,6},{8,15},{9,8},{10,9... | collective-permute-start | bytes 2408456 | tf_op jit(solution)/shard_map/ppermute | solution.py:589
  13.6 0.0 collective-permute-done.1
  13.6 0.8 pad_maximum_fusion
  14.4 1.6 %collective-permute-start.2 = (f32[128,256]{1,0:T(8,128)S(1)}, f32[128,256]{1,0:T(8,128)S(1)}, u32[]{:S(2)}, u32[]{:S(2)}) collective-permute-start(f32[128,256]{1,0:T(8,128)S(1)} %pad_maximum_fusion), channel_id=1, source_target_pairs={{0,16},{8,24},{16,0},{24,8},{1,17},{9,25},{17,1},{25,9},{2,18},{10... | collective-permute-start | bytes 393224 | tf_op jit(solution)/shard_map/ppermute | solution.py:591
  16.0 1.5 %constant_dynamic-update-slice_fusion.2 = f32[256,256]{1,0:T(8,128)} fusion(f32[64,256]{1,0:T(8,128)} %get-tuple-element.37), kind=kLoop, calls=%fused_computation.3 | loop fusion | bytes 131072
  17.5 1.7 %collective-permute-start.5 = (f32[1296,256]{1,0:T(8,128)}, f32[1296,256]{1,0:T(8,128)}, u32[]{:S(2)}, u32[]{:S(2)}) collective-permute-start(f32[1296,256]{1,0:T(8,128)} %get-tuple-element.46), channel_id=1, source_target_pairs={{8,16},{16,8},{9,17},{17,9},{10,18},{18,10},{11,19},{19,11},{12,20... | collective-permute-start | bytes 3981320 | tf_op jit(solution)/shard_map/ppermute | solution.py:586
  19.2 0.6 constant_dynamic-update-slice_fusion.1
  19.8 0.7 constant_dynamic-update-slice_fusion.refs_2_
  20.5 0.0 collective-permute-start.6
  20.5 3.8 %collective-permute-start.7 = (f32[256,256]{1,0:T(8,128)}, f32[256,256]{1,0:T(8,128)}, u32[]{:S(2)}, u32[]{:S(2)}) collective-permute-start(f32[256,256]{1,0:T(8,128)} %constant_dynamic-update-slice_fusion.refs_2_), channel_id=1, source_target_pairs={{0,6},{1,7},{2,0},{3,1},{4,2},{5,3},{6,4},{7,5},{8,14},{9,15},{10,... | collective-permute-start | bytes 786440 | tf_op jit(solution)/shard_map/ppermute | solution.py:595
  24.3 13.4 %own.1.before = f32[4,512,256]{2,1,0:T(8,128)} custom-call(s32[4,9]{1,0:T(4,128)} %bitcast.19, f32[4,8,512]{2,1,0:T(8,128)} %get-tuple-element.41.place8, f32[4,512,256]{2,1,0:T(8,128)} %bitcast.26, f32[784,256]{1,0:T(8,128)} %get-tuple-element.42.msg.own), custom_call_target="tpu_custom_call" | custom-call | flops 20000000000 | bytes 4000000 | tf_op jit(solution)/shard_map/own/pallas_call | solution.py:334
  37.7 2.4 %collective-permute-done.6.refs_3_ = f32[256,256]{1,0:T(8,128)} collective-permute-done((f32[256,256]{1,0:T(8,128)}, f32[256,256]{1,0:T(8,128)}, u32[]{:S(2)}, u32[]{:S(2)}) %collective-permute-start.6) | collective-permute-done | bytes 262176 | tf_op jit(solution)/shard_map/ppermute | solution.py:595
  40.1 2.5 %collective-permute-done.7.refs_5_ = f32[256,256]{1,0:T(8,128)} collective-permute-done((f32[256,256]{1,0:T(8,128)}, f32[256,256]{1,0:T(8,128)}, u32[]{:S(2)}, u32[]{:S(2)}) %collective-permute-start.7) | collective-permute-done | bytes 262176 | tf_op jit(solution)/shard_map/ppermute | solution.py:595
  42.6 2.6 %collective-permute-start.12 = (f32[256,256]{1,0:T(8,128)}, f32[256,256]{1,0:T(8,128)}, u32[]{:S(2)}, u32[]{:S(2)}) collective-permute-start(f32[256,256]{1,0:T(8,128)} %constant_dynamic-update-slice_fusion.refs_2_), channel_id=1, source_target_pairs={{0,4},{1,5},{2,6},{3,7},{4,0},{5,1},{6,2},{7,3},{8,12},{9,13},{10,... | collective-permute-start | bytes 786440 | tf_op jit(solution)/shard_map/ppermute | solution.py:595
  45.2 8.4 %lat.1.before = f32[4,512,256]{2,1,0:T(8,128)} custom-call(s32[4,9]{1,0:T(4,128)} %bitcast.20, f32[4,8,512]{2,1,0:T(8,128)} %get-tuple-element.41.place8, f32[1296,256]{1,0:T(8,128)} %collective-permute-done.5.from_y, f32[1296,256]{1,0:T(8,128)} %collective-permute-done.from_c, f32[4,512,256]{2,1,0:T(8,128)} %own.1.before), custom_call_target="tpu_custom_call", output_to_operand_aliasing={{}: (4, {})} | custom-call | flops 20000000000 | bytes 4000000 | tf_op jit(solution)/shard_map/lat/pallas_call | solution.py:334
  53.7 1.6 %collective-permute-start.10 = (f32[784,256]{1,0:T(8,128)}, f32[784,256]{1,0:T(8,128)}, u32[]{:S(2)}, u32[]{:S(2)}) collective-permute-start(f32[784,256]{1,0:T(8,128)} %collective-permute-done.3.refs_0_.left.a_left), channel_id=1, source_target_pairs={{8,16},{16,8},{9,17},{17,9},{10,18},{18,10},{11,19},{19,11},{12,20... | collective-permute-start | bytes 2408456 | tf_op jit(solution)/shard_map/ppermute | solution.py:606
  55.3 1.5 %collective-permute-start.11 = (f32[784,256]{1,0:T(8,128)}, f32[784,256]{1,0:T(8,128)}, u32[]{:S(2)}, u32[]{:S(2)}) collective-permute-start(f32[784,256]{1,0:T(8,128)} %collective-permute-done.4.refs_1_.right.a_right), channel_id=1, source_target_pairs={{8,16},{16,8},{9,17},{17,9},{10,18},{18,10},{11,19},{19,11},{12,20... | collective-permute-start | bytes 2408456 | tf_op jit(solution)/shard_map/ppermute | solution.py:607
  56.8 4.7 %collective-permute-start.9 = (f32[512,256]{1,0:T(8,128)}, f32[512,256]{1,0:T(8,128)}, u32[]{:S(2)}, u32[]{:S(2)}) collective-permute-start(f32[512,256]{1,0:T(8,128)} %get-tuple-element.54), channel_id=1, source_target_pairs={{0,7},{1,0},{2,1},{3,2},{4,3},{5,4},{6,5},{7,6},{8,15},{9,8},{10,9... | collective-permute-start | bytes 1572872 | tf_op jit(solution)/shard_map/ppermute | solution.py:605
  61.5 2.5 %pack.1.devices = f32[1568,256]{1,0:T(8,128)} custom-call(f32[784,256]{1,0:T(8,128)} %collective-permute-done.3.refs_0_.left.a_left, f32[784,256]{1,0:T(8,128)} %collective-permute-done.4.refs_1_.right.a_right, f32[256,256]{1,0:T(8,128)} %constant_dynamic-update-slice_fusion.refs_2_, f32[256,256]{1,0:T(8,128)} %collective-permute-done.6.refs_3_, ...), custom_call_target="tpu_custom_call" | custom-call | flops 1000 | bytes 1000 | tf_op jit(solution)/shard_map/pack/pallas_call | solution.py:503
  64.1 1.7 %collective-permute-start.13 = (f32[1568,256]{1,0:T(8,128)}, f32[1568,256]{1,0:T(8,128)}, u32[]{:S(2)}, u32[]{:S(2)}) collective-permute-start(f32[1568,256]{1,0:T(8,128)} %pack.1.devices), channel_id=1, source_target_pairs={{0,8},{8,0},{16,24},{24,16},{1,9},{9,1},{17,25},{25,17},{2,10},{10... | collective-permute-start | bytes 4816904 | tf_op jit(solution)/shard_map/ppermute | solution.py:609
  65.8 7.0 %lon.1.before = f32[4,512,256]{2,1,0:T(8,128)} custom-call(s32[4,9]{1,0:T(4,128)} %bitcast.21, f32[4,8,512]{2,1,0:T(8,128)} %get-tuple-element.41.place8, f32[784,256]{1,0:T(8,128)} %collective-permute-done.3.refs_0_.left.a_left, f32[784,256]{1,0:T(8,128)} %collective-permute-done.4.refs_1_.right.a_right, ...), custom_call_target="tpu_custom_call", output_to_operand_aliasing={{}: (4, {})} | custom-call | flops 20000000000 | bytes 4000000 | tf_op jit(solution)/shard_map/lon/pallas_call | solution.py:334
  72.8 7.1 %far.1.partial = f32[256,256]{1,0:T(8,128)} custom-call(s32[4,9]{1,0:T(4,128)} %bitcast.22, bf16[4,36,64,64]{3,2,1,0:T(8,128)(2,1)} %bitcast.11, f32[784,256]{1,0:T(8,128)} %get-tuple-element.42.msg.own, f32[784,256]{1,0:T(8,128)} %collective-permute-done.3.refs_0_.left.a_left, f32[784,256]{1,0:T(8,128)} %collective-permute-done.4.refs_1_.right.a_right, ...), custom_call_target="tpu_custom_call" | custom-call | flops 1000 | bytes 1000 | tf_op jit(solution)/shard_map/far/pallas_call | solution.py:465
  79.9 7.5 %down.1.before = f32[4,512,256]{2,1,0:T(8,128)} custom-call(s32[4,9]{1,0:T(4,128)} %bitcast.23, f32[4,8,512]{2,1,0:T(8,128)} %get-tuple-element.41.place8, bf16[4,36,64,64]{3,2,1,0:T(8,128)(2,1)} %bitcast.12, f32[784,256]{1,0:T(8,128)} %collective-permute-done.10.left_y, f32[784,256]{1,0:T(8,128)} %collective-permute-done.11.right_y, ...), custom_call_target="tpu_custom_call", output_to_operand_aliasing={{}: (7, {})} | custom-call | flops 1000 | bytes 1000 | tf_op jit(solution)/shard_map/down/pallas_call | solution.py:334
  87.4 1.8 %collective-permute-start.14 = (f32[512,256]{1,0:T(8,128)}, f32[512,256]{1,0:T(8,128)}, u32[]{:S(2)}, u32[]{:S(2)}) collective-permute-start(f32[512,256]{1,0:T(8,128)} %collective-permute-done.8.left), channel_id=1, source_target_pairs={{0,8},{8,0},{16,24},{24,16},{1,9},{9,1},{17,25},{25,17},{2,10},{10... | collective-permute-start | bytes 1572872 | tf_op jit(solution)/shard_map/ppermute | solution.py:647
  89.2 0.1 collective-permute-start.15
  89.3 1.8 %collective-permute-done.14.left_c = f32[512,256]{1,0:T(8,128)} collective-permute-done((f32[512,256]{1,0:T(8,128)}, f32[512,256]{1,0:T(8,128)}, u32[]{:S(2)}, u32[]{:S(2)}) %collective-permute-start.14) | collective-permute-done | bytes 524320 | tf_op jit(solution)/shard_map/ppermute | solution.py:647
  91.1 0.7 collective-permute-done.15.right_c
  91.8 6.3 %last.1 = f32[4,512,256]{2,1,0:T(8,128)} custom-call(s32[4,9]{1,0:T(4,128)} %bitcast.24, f32[4,8,512]{2,1,0:T(8,128)} %get-tuple-element.41.place8, f32[784,256]{1,0:T(8,128)} %collective-permute-done.3.refs_0_.left.a_left, f32[784,256]{1,0:T(8,128)} %collective-permute-done.4.refs_1_.right.a_right, ...), custom_call_target="tpu_custom_call", output_to_operand_aliasing={{}: (9, {})} | custom-call | flops 20000000000 | bytes 4000000 | tf_op jit(solution)/shard_map/last/pallas_call | solution.py:334
  (12 shorter events, 0.0 us)
Async XLA Ops:
  5.8 14.7 %collective-permute-start = (f32[1296,256]{1,0:T(8,128)}, f32[1296,256]{1,0:T(8,128)}, u32[]{:S(2)}, u32[]{:S(2)}) collective-permute-start(f32[1296,256]{1,0:T(8,128)} %get-tuple-element.36), channel_id=1, source_target_pairs={{0,8},{8,0},{16,24},{24,16},{1,9},{9,1},{17,25},{25,17},{2,10},{10... | collective-permute-start | bytes 3981320 | tf_op jit(solution)/shard_map/ppermute | solution.py:584
  6.3 7.3 %collective-permute-start.1 = (f32[64,256]{1,0:T(8,128)}, f32[64,256]{1,0:T(8,128)S(1)}, u32[]{:S(2)}, u32[]{:S(2)}) collective-permute-start(f32[64,256]{1,0:T(8,128)} %get-tuple-element.37), channel_id=1, source_target_pairs={{0,1},{1,0},{2,3},{3,2},{4,5},{5,4},{6,7},{7,6},{8,9},{9,8},{10,11... | collective-permute-start | bytes 196616 | tf_op jit(solution)/shard_map/ppermute | solution.py:583
  8.8 44.8 %collective-permute-start.3 = (f32[784,256]{1,0:T(8,128)}, f32[784,256]{1,0:T(8,128)}, u32[]{:S(2)}, u32[]{:S(2)}) collective-permute-start(f32[784,256]{1,0:T(8,128)} %get-tuple-element.42.msg.own), channel_id=1, source_target_pairs={{0,1},{1,2},{2,3},{3,4},{4,5},{5,6},{6,7},{7,0},{8,9},{9,10},{10,1... | collective-permute-start | bytes 2408456 | tf_op jit(solution)/shard_map/ppermute | solution.py:588
  8.9 44.7 %collective-permute-start.4 = (f32[784,256]{1,0:T(8,128)}, f32[784,256]{1,0:T(8,128)}, u32[]{:S(2)}, u32[]{:S(2)}) collective-permute-start(f32[784,256]{1,0:T(8,128)} %get-tuple-element.43), channel_id=1, source_target_pairs={{0,7},{1,0},{2,1},{3,2},{4,3},{5,4},{6,5},{7,6},{8,15},{9,8},{10,9... | collective-permute-start | bytes 2408456 | tf_op jit(solution)/shard_map/ppermute | solution.py:589
  14.4 5.4 %collective-permute-start.2 = (f32[128,256]{1,0:T(8,128)S(1)}, f32[128,256]{1,0:T(8,128)S(1)}, u32[]{:S(2)}, u32[]{:S(2)}) collective-permute-start(f32[128,256]{1,0:T(8,128)S(1)} %pad_maximum_fusion), channel_id=1, source_target_pairs={{0,16},{8,24},{16,0},{24,8},{1,17},{9,25},{17,1},{25,9},{2,18},{10... | collective-permute-start | bytes 393224 | tf_op jit(solution)/shard_map/ppermute | solution.py:591
  17.5 25.1 %collective-permute-start.5 = (f32[1296,256]{1,0:T(8,128)}, f32[1296,256]{1,0:T(8,128)}, u32[]{:S(2)}, u32[]{:S(2)}) collective-permute-start(f32[1296,256]{1,0:T(8,128)} %get-tuple-element.46), channel_id=1, source_target_pairs={{8,16},{16,8},{9,17},{17,9},{10,18},{18,10},{11,19},{19,11},{12,20... | collective-permute-start | bytes 3981320 | tf_op jit(solution)/shard_map/ppermute | solution.py:586
  20.5 19.6 %collective-permute-start.6 = (f32[256,256]{1,0:T(8,128)}, f32[256,256]{1,0:T(8,128)}, u32[]{:S(2)}, u32[]{:S(2)}) collective-permute-start(f32[256,256]{1,0:T(8,128)} %constant_dynamic-update-slice_fusion.refs_2_), channel_id=1, source_target_pairs={{0,2},{1,3},{2,4},{3,5},{4,6},{5,7},{6,0},{7,1},{8,10},{9,11},{10,... | collective-permute-start | bytes 786440 | tf_op jit(solution)/shard_map/ppermute | solution.py:595
  20.5 22.1 %collective-permute-start.7 = (f32[256,256]{1,0:T(8,128)}, f32[256,256]{1,0:T(8,128)}, u32[]{:S(2)}, u32[]{:S(2)}) collective-permute-start(f32[256,256]{1,0:T(8,128)} %constant_dynamic-update-slice_fusion.refs_2_), channel_id=1, source_target_pairs={{0,6},{1,7},{2,0},{3,1},{4,2},{5,3},{6,4},{7,5},{8,14},{9,15},{10,... | collective-permute-start | bytes 786440 | tf_op jit(solution)/shard_map/ppermute | solution.py:595
  42.6 19.0 %collective-permute-start.12 = (f32[256,256]{1,0:T(8,128)}, f32[256,256]{1,0:T(8,128)}, u32[]{:S(2)}, u32[]{:S(2)}) collective-permute-start(f32[256,256]{1,0:T(8,128)} %constant_dynamic-update-slice_fusion.refs_2_), channel_id=1, source_target_pairs={{0,4},{1,5},{2,6},{3,7},{4,0},{5,1},{6,2},{7,3},{8,12},{9,13},{10,... | collective-permute-start | bytes 786440 | tf_op jit(solution)/shard_map/ppermute | solution.py:595
  53.7 26.2 %collective-permute-start.10 = (f32[784,256]{1,0:T(8,128)}, f32[784,256]{1,0:T(8,128)}, u32[]{:S(2)}, u32[]{:S(2)}) collective-permute-start(f32[784,256]{1,0:T(8,128)} %collective-permute-done.3.refs_0_.left.a_left), channel_id=1, source_target_pairs={{8,16},{16,8},{9,17},{17,9},{10,18},{18,10},{11,19},{19,11},{12,20... | collective-permute-start | bytes 2408456 | tf_op jit(solution)/shard_map/ppermute | solution.py:606
  55.3 24.6 %collective-permute-start.11 = (f32[784,256]{1,0:T(8,128)}, f32[784,256]{1,0:T(8,128)}, u32[]{:S(2)}, u32[]{:S(2)}) collective-permute-start(f32[784,256]{1,0:T(8,128)} %collective-permute-done.4.refs_1_.right.a_right), channel_id=1, source_target_pairs={{8,16},{16,8},{9,17},{17,9},{10,18},{18,10},{11,19},{19,11},{12,20... | collective-permute-start | bytes 2408456 | tf_op jit(solution)/shard_map/ppermute | solution.py:607
  56.8 30.5 %collective-permute-start.8 = (f32[512,256]{1,0:T(8,128)}, f32[512,256]{1,0:T(8,128)}, u32[]{:S(2)}, u32[]{:S(2)}) collective-permute-start(f32[512,256]{1,0:T(8,128)} %get-tuple-element.53), channel_id=1, source_target_pairs={{0,1},{1,2},{2,3},{3,4},{4,5},{5,6},{6,7},{7,0},{8,9},{9,10},{10,1... | collective-permute-start | bytes 1572872 | tf_op jit(solution)/shard_map/ppermute | solution.py:604
  56.8 30.5 %collective-permute-start.9 = (f32[512,256]{1,0:T(8,128)}, f32[512,256]{1,0:T(8,128)}, u32[]{:S(2)}, u32[]{:S(2)}) collective-permute-start(f32[512,256]{1,0:T(8,128)} %get-tuple-element.54), channel_id=1, source_target_pairs={{0,7},{1,0},{2,1},{3,2},{4,3},{5,4},{6,5},{7,6},{8,15},{9,8},{10,9... | collective-permute-start | bytes 1572872 | tf_op jit(solution)/shard_map/ppermute | solution.py:605
  64.1 8.6 %collective-permute-start.13 = (f32[1568,256]{1,0:T(8,128)}, f32[1568,256]{1,0:T(8,128)}, u32[]{:S(2)}, u32[]{:S(2)}) collective-permute-start(f32[1568,256]{1,0:T(8,128)} %pack.1.devices), channel_id=1, source_target_pairs={{0,8},{8,0},{16,24},{24,16},{1,9},{9,1},{17,25},{25,17},{2,10},{10... | collective-permute-start | bytes 4816904 | tf_op jit(solution)/shard_map/ppermute | solution.py:609
  87.4 3.7 %collective-permute-start.14 = (f32[512,256]{1,0:T(8,128)}, f32[512,256]{1,0:T(8,128)}, u32[]{:S(2)}, u32[]{:S(2)}) collective-permute-start(f32[512,256]{1,0:T(8,128)} %collective-permute-done.8.left), channel_id=1, source_target_pairs={{0,8},{8,0},{16,24},{24,16},{1,9},{9,1},{17,25},{25,17},{2,10},{10... | collective-permute-start | bytes 1572872 | tf_op jit(solution)/shard_map/ppermute | solution.py:647
  89.2 2.6 %collective-permute-start.15 = (f32[512,256]{1,0:T(8,128)}, f32[512,256]{1,0:T(8,128)}, u32[]{:S(2)}, u32[]{:S(2)}) collective-permute-start(f32[512,256]{1,0:T(8,128)} %collective-permute-done.9.right), channel_id=1, source_target_pairs={{0,8},{8,0},{16,24},{24,16},{1,9},{9,1},{17,25},{25,17},{2,10},{10... | collective-permute-start | bytes 1572872 | tf_op jit(solution)/shard_map/ppermute | solution.py:648
where the time goes:
time: 97.5 us; the launch traced here: 98.3 us
  Pallas kernels  57.9 us (59%)
  starting transfers between devices  29 us (30%)
  waiting for transfers between devices  7.48 us (8%)
  local copies, waits for them, and re-layouts  2.73 us (3%)
    pallas_call x5, Pallas kernels, near(): pl.pallas_call(kernel, in_specs=[scalars, whole] + [hbm] * (len(operands)...  42.6 us
    pallas_call x1, Pallas kernels, far_field(): pl.pallas_call(functools.partial(far_kernel, n_lat, n_lon), in_specs=[sca...  7.08 us
    ppermute x3, starting transfers between devices, rotate(): lax.ppermute(quad, 'lon', [(i, (i + step) % n_lon) for i in range(n_lon)])  6.46 us
    pallas_call x1, Pallas kernels, coefficients(): pl.pallas_call(coef_kernel, in_specs=[hbm, hbm, whole, whole], out_specs=...  5.75 us
    ppermute x3, waiting for transfers between devices, rotate(): lax.ppermute(quad, 'lon', [(i, (i + step) % n_lon) for i in range(n_lon)])  4.9 us
    ppermute x1, starting transfers between devices, local(): right_b = lax.ppermute(b_left, 'lon', to_left)  4.72 us
    ppermute x1, starting transfers between devices, local(): right = lax.ppermute(a_left, 'lon', to_left)  4.64 us
    ppermute x1, starting transfers between devices, local(): dev_pair = lax.ppermute(dev, 'lon', partner)  2.57 us
  transfers between devices with their start and end apart: 16, of which 4 were waited for; matrix products, arithmetic and copies ran while one was open for 4% of the time, Pallas kernels for 47%

commit v1 on v0

--- a/solution.py
+++ b/solution.py
@@ -597,9 +597,9 @@
     first, last = rotate(2), rotate(n_lon - 2)
     from_c, quad, place8 = barrier((from_c, quad, place8))
     (acc,) = near(own_kernel, "own", 4, 16, (flags, place8, flat, a_right), chained=False)
-    from_y, first, last, quad, acc = barrier((from_y, first, last, quad, acc))
+    from_y, quad, acc = barrier((from_y, quad, acc))
     moved = [first, *(rotate(step) for step in range(4, n_lon - 2, 2)), last]
-    (acc,) = near(lat_kernel, "lat", 4, 8, (flags, place8, from_y, from_c, acc))
+    (acc,) = near(lat_kernel, "lat", 4, 8, (flags, place8, from_y, from_c, acc), cost=LOW)
     left, right, b_right, b_left, acc = barrier((left, right, b_right, b_left, acc))
     left_b = lax.ppermute(b_right, "lon", to_right)
     right_b = lax.ppermute(b_left, "lon", to_left)
@@ -628,7 +628,11 @@
             transfer,
         ),
     )
-    left_y, right_y, partial = barrier((left_y, right_y, partial))
+    left_b, right_b, left_y, right_y, partial = barrier(
+        (left_b, right_b, left_y, right_y, partial)
+    )
+    left_c = lax.ppermute(left_b, "lat", in_chip)
+    right_c = lax.ppermute(right_b, "lat", in_chip)
     (acc,) = near(
         down_kernel,
         "down",
@@ -643,9 +647,7 @@
             pltpu.SemaphoreType.DMA((5,)),
         ],
     )
-    left_b, right_b, acc = barrier((left_b, right_b, acc))
-    left_c = lax.ppermute(left_b, "lat", in_chip)
-    right_c = lax.ppermute(right_b, "lat", in_chip)
+    left_c, right_c, acc = barrier((left_c, right_c, acc))
     (acc,) = near(
         last_kernel,
         "last",

time: 97.5 us -> 92.7 us (0.951)
  the two profiles are of different devices: /device:TPU:0 before, /device:TPU:9 now
where the time goes in v1:
time: 92.7 us; the launch traced here: 91.7 us
  Pallas kernels  53.6 us (58%)
  starting transfers between devices  21.4 us (23%)
  waiting for transfers between devices  12.9 us (14%)
  local copies, waits for them, and re-layouts  2.74 us (3%)
    pallas_call x5, Pallas kernels, near(): pl.pallas_call(kernel, in_specs=[scalars, whole] + [hbm] * (len(operands)...  38.2 us
    pallas_call x1, Pallas kernels, far_field(): pl.pallas_call(functools.partial(far_kernel, n_lat, n_lon), in_specs=[sca...  7.08 us
    pallas_call x1, Pallas kernels, coefficients(): pl.pallas_call(coef_kernel, in_specs=[hbm, hbm, whole, whole], out_specs=...  5.72 us
    ppermute x3, starting transfers between devices, rotate(): lax.ppermute(quad, 'lon', [(i, (i + step) % n_lon) for i in range(n_lon)])  4.05 us
    ppermute x1, waiting for transfers between devices, local(): left_b = lax.ppermute(b_right, 'lon', to_right)  4.04 us
    ppermute x1, starting transfers between devices, local(): left_y = lax.ppermute(left, 'lat', across)  3.49 us
    ppermute x1, starting transfers between devices, local(): from_y = lax.ppermute(to_y, 'lat', across)  3.14 us
    pallas_call x1, Pallas kernels, pack(): pl.pallas_call(pack_kernel, in_specs=[hbm] * len(parts), out_specs=whole,...  2.55 us
  transfers between devices with their start and end apart: 16, of which 6 were waited for; matrix products, arithmetic and copies ran while one was open for 4% of the time, Pallas kernels for 44%

profile of v1, /device:TPU:9, one launch (start us, length us, event | category | flops | bytes accessed | tf_op | source)
XLA Modules:
  0.0 91.7 jit_solution(16153933149931983618)
XLA Ops:
  0.0 5.7 %coefs.1 = (f32[784,256]{1,0:T(8,128)}, f32[784,256]{1,0:T(8,128)}, f32[512,256]{1,0:T(8,128)}, f32[512,256]{1,0:T(8,128)}, f32[1296,256]{1,0:T(8,128)}, /*index...) custom-call(f32[4,512,256]{2,1,0:T(8,128)} %bitcast.25, f32[4,64,512]{2,1,0:T(8,128)} %bitcast.15, ...), custom_call_target="tpu_custom_call" | custom-call | flops 20000000000 | bytes 4000000 | tf_op jit(solution)/shard_map/coefs/pallas_call | solution.py:130
  5.7 0.7 collective-permute-start
  6.5 1.2 %collective-permute-start.1 = (f32[64,256]{1,0:T(8,128)}, f32[64,256]{1,0:T(8,128)S(1)}, u32[]{:S(2)}, u32[]{:S(2)}) collective-permute-start(f32[64,256]{1,0:T(8,128)} %get-tuple-element.37), channel_id=1, source_target_pairs={{0,1},{1,0},{2,3},{3,2},{4,5},{5,4},{6,7},{7,6},{8,9},{9,8},{10,11... | collective-permute-start | bytes 196616 | tf_op jit(solution)/shard_map/ppermute | solution.py:583
  7.7 0.3 collective-permute-start.3
  8.0 2.1 %collective-permute-start.4 = (f32[784,256]{1,0:T(8,128)}, f32[784,256]{1,0:T(8,128)}, u32[]{:S(2)}, u32[]{:S(2)}) collective-permute-start(f32[784,256]{1,0:T(8,128)} %get-tuple-element.43), channel_id=1, source_target_pairs={{0,7},{1,0},{2,1},{3,2},{4,3},{5,4},{6,5},{7,6},{8,15},{9,8},{10,9... | collective-permute-start | bytes 2408456 | tf_op jit(solution)/shard_map/ppermute | solution.py:589
  10.1 0.3 collective-permute-done.1
  10.4 0.8 pad_maximum_fusion
  11.2 1.3 %collective-permute-start.2 = (f32[128,256]{1,0:T(8,128)S(1)}, f32[128,256]{1,0:T(8,128)S(1)}, u32[]{:S(2)}, u32[]{:S(2)}) collective-permute-start(f32[128,256]{1,0:T(8,128)S(1)} %pad_maximum_fusion), channel_id=1, source_target_pairs={{0,16},{8,24},{16,0},{24,8},{1,17},{9,25},{17,1},{25,9},{2,18},{10... | collective-permute-start | bytes 393224 | tf_op jit(solution)/shard_map/ppermute | solution.py:591
  12.5 1.5 %constant_dynamic-update-slice_fusion.2 = f32[256,256]{1,0:T(8,128)} fusion(f32[64,256]{1,0:T(8,128)} %get-tuple-element.37), kind=kLoop, calls=%fused_computation.3 | loop fusion | bytes 131072
  14.0 3.1 %collective-permute-start.5 = (f32[1296,256]{1,0:T(8,128)}, f32[1296,256]{1,0:T(8,128)}, u32[]{:S(2)}, u32[]{:S(2)}) collective-permute-start(f32[1296,256]{1,0:T(8,128)} %get-tuple-element.46), channel_id=1, source_target_pairs={{8,16},{16,8},{9,17},{17,9},{10,18},{18,10},{11,19},{19,11},{12,20... | collective-permute-start | bytes 3981320 | tf_op jit(solution)/shard_map/ppermute | solution.py:586
  17.1 0.6 constant_dynamic-update-slice_fusion.1
  17.7 0.7 constant_dynamic-update-slice_fusion.refs_2_
  18.4 1.3 %collective-permute-start.10 = (f32[256,256]{1,0:T(8,128)}, f32[256,256]{1,0:T(8,128)}, u32[]{:S(2)}, u32[]{:S(2)}) collective-permute-start(f32[256,256]{1,0:T(8,128)} %constant_dynamic-update-slice_fusion.refs_2_), channel_id=1, source_target_pairs={{0,2},{1,3},{2,4},{3,5},{4,6},{5,7},{6,0},{7,1},{8,10},{9,11},{10,... | collective-permute-start | bytes 786440 | tf_op jit(solution)/shard_map/ppermute | solution.py:595
  19.7 0.4 collective-permute-start.12
  20.2 11.6 %own.1.before = f32[4,512,256]{2,1,0:T(8,128)} custom-call(s32[4,9]{1,0:T(4,128)} %bitcast.19, f32[4,8,512]{2,1,0:T(8,128)} %get-tuple-element.41.place8, f32[4,512,256]{2,1,0:T(8,128)} %bitcast.26, f32[784,256]{1,0:T(8,128)} %get-tuple-element.42.msg.own), custom_call_target="tpu_custom_call" | custom-call | flops 20000000000 | bytes 4000000 | tf_op jit(solution)/shard_map/own/pallas_call | solution.py:334
  31.8 1.9 %collective-permute-done.5.from_y = f32[1296,256]{1,0:T(8,128)} collective-permute-done((f32[1296,256]{1,0:T(8,128)}, f32[1296,256]{1,0:T(8,128)}, u32[]{:S(2)}, u32[]{:S(2)}) %collective-permute-start.5) | collective-permute-done | bytes 1327136 | tf_op jit(solution)/shard_map/ppermute | solution.py:586
  33.7 2.3 %collective-permute-start.11 = (f32[256,256]{1,0:T(8,128)}, f32[256,256]{1,0:T(8,128)}, u32[]{:S(2)}, u32[]{:S(2)}) collective-permute-start(f32[256,256]{1,0:T(8,128)} %constant_dynamic-update-slice_fusion.refs_2_), channel_id=1, source_target_pairs={{0,4},{1,5},{2,6},{3,7},{4,0},{5,1},{6,2},{7,3},{8,12},{9,13},{10,... | collective-permute-start | bytes 786440 | tf_op jit(solution)/shard_map/ppermute | solution.py:595
  36.0 5.8 %lat.1.before = f32[4,512,256]{2,1,0:T(8,128)} custom-call(s32[4,9]{1,0:T(4,128)} %bitcast.20, f32[4,8,512]{2,1,0:T(8,128)} %get-tuple-element.41.place8, f32[1296,256]{1,0:T(8,128)} %collective-permute-done.5.from_y, f32[1296,256]{1,0:T(8,128)} %collective-permute-done.from_c, f32[4,512,256]{2,1,0:T(8,128)} %own.1.before), custom_call_target="tpu_custom_call", output_to_operand_aliasing={{}: (4, {})} | custom-call | flops 1000 | bytes 1000 | tf_op jit(solution)/shard_map/lat/pallas_call | solution.py:334
  41.8 2.1 %collective-permute-done.3.refs_0_.left.a_left = f32[784,256]{1,0:T(8,128)} collective-permute-done((f32[784,256]{1,0:T(8,128)}, f32[784,256]{1,0:T(8,128)}, u32[]{:S(2)}, u32[]{:S(2)}) %collective-permute-start.3) | collective-permute-done | bytes 802848 | tf_op jit(solution)/shard_map/ppermute | solution.py:588
  43.9 2.1 %collective-permute-done.4.refs_1_.right.a_right = f32[784,256]{1,0:T(8,128)} collective-permute-done((f32[784,256]{1,0:T(8,128)}, f32[784,256]{1,0:T(8,128)}, u32[]{:S(2)}, u32[]{:S(2)}) %collective-permute-start.4) | collective-permute-done | bytes 802848 | tf_op jit(solution)/shard_map/ppermute | solution.py:589
  46.0 3.5 %collective-permute-start.8 = (f32[784,256]{1,0:T(8,128)}, f32[784,256]{1,0:T(8,128)}, u32[]{:S(2)}, u32[]{:S(2)}) collective-permute-start(f32[784,256]{1,0:T(8,128)} %collective-permute-done.3.refs_0_.left.a_left), channel_id=1, source_target_pairs={{8,16},{16,8},{9,17},{17,9},{10,18},{18,10},{11,19},{19,11},{12,20... | collective-permute-start | bytes 2408456 | tf_op jit(solution)/shard_map/ppermute | solution.py:606
  49.5 2.1 %collective-permute-start.9 = (f32[784,256]{1,0:T(8,128)}, f32[784,256]{1,0:T(8,128)}, u32[]{:S(2)}, u32[]{:S(2)}) collective-permute-start(f32[784,256]{1,0:T(8,128)} %collective-permute-done.4.refs_1_.right.a_right), channel_id=1, source_target_pairs={{8,16},{16,8},{9,17},{17,9},{10,18},{18,10},{11,19},{19,11},{12,20... | collective-permute-start | bytes 2408456 | tf_op jit(solution)/shard_map/ppermute | solution.py:607
  51.5 1.2 %collective-permute-start.6 = (f32[512,256]{1,0:T(8,128)}, f32[512,256]{1,0:T(8,128)}, u32[]{:S(2)}, u32[]{:S(2)}) collective-permute-start(f32[512,256]{1,0:T(8,128)} %get-tuple-element.53), channel_id=1, source_target_pairs={{0,1},{1,2},{2,3},{3,4},{4,5},{5,6},{6,7},{7,0},{8,9},{9,10},{10,1... | collective-permute-start | bytes 1572872 | tf_op jit(solution)/shard_map/ppermute | solution.py:604
  52.7 1.2 %collective-permute-start.7 = (f32[512,256]{1,0:T(8,128)}, f32[512,256]{1,0:T(8,128)}, u32[]{:S(2)}, u32[]{:S(2)}) collective-permute-start(f32[512,256]{1,0:T(8,128)} %get-tuple-element.54), channel_id=1, source_target_pairs={{0,7},{1,0},{2,1},{3,2},{4,3},{5,4},{6,5},{7,6},{8,15},{9,8},{10,9... | collective-permute-start | bytes 1572872 | tf_op jit(solution)/shard_map/ppermute | solution.py:605
  54.0 2.5 %pack.1.devices = f32[1568,256]{1,0:T(8,128)} custom-call(f32[784,256]{1,0:T(8,128)} %collective-permute-done.3.refs_0_.left.a_left, f32[784,256]{1,0:T(8,128)} %collective-permute-done.4.refs_1_.right.a_right, f32[256,256]{1,0:T(8,128)} %constant_dynamic-update-slice_fusion.refs_2_, f32[256,256]{1,0:T(8,128)} %collective-permute-done.10.refs_3_, ...), custom_call_target="tpu_custom_call" | custom-call | flops 1000 | bytes 1000 | tf_op jit(solution)/shard_map/pack/pallas_call | solution.py:503
  56.6 6.1 %lon.1.before = f32[4,512,256]{2,1,0:T(8,128)} custom-call(s32[4,9]{1,0:T(4,128)} %bitcast.21, f32[4,8,512]{2,1,0:T(8,128)} %get-tuple-element.41.place8, f32[784,256]{1,0:T(8,128)} %collective-permute-done.3.refs_0_.left.a_left, f32[784,256]{1,0:T(8,128)} %collective-permute-done.4.refs_1_.right.a_right, ...), custom_call_target="tpu_custom_call", output_to_operand_aliasing={{}: (4, {})} | custom-call | flops 20000000000 | bytes 4000000 | tf_op jit(solution)/shard_map/lon/pallas_call | solution.py:334
  62.7 7.1 %far.1.partial = f32[256,256]{1,0:T(8,128)} custom-call(s32[4,9]{1,0:T(4,128)} %bitcast.22, bf16[4,36,64,64]{3,2,1,0:T(8,128)(2,1)} %bitcast.11, f32[784,256]{1,0:T(8,128)} %get-tuple-element.42.msg.own, f32[784,256]{1,0:T(8,128)} %collective-permute-done.3.refs_0_.left.a_left, f32[784,256]{1,0:T(8,128)} %collective-permute-done.4.refs_1_.right.a_right, ...), custom_call_target="tpu_custom_call" | custom-call | flops 1000 | bytes 1000 | tf_op jit(solution)/shard_map/far/pallas_call | solution.py:465
  69.8 4.0 %collective-permute-done.6.left = f32[512,256]{1,0:T(8,128)} collective-permute-done((f32[512,256]{1,0:T(8,128)}, f32[512,256]{1,0:T(8,128)}, u32[]{:S(2)}, u32[]{:S(2)}) %collective-permute-start.6) | collective-permute-done | bytes 524320 | tf_op jit(solution)/shard_map/ppermute | solution.py:604
  73.9 2.5 %collective-permute-done.7.right = f32[512,256]{1,0:T(8,128)} collective-permute-done((f32[512,256]{1,0:T(8,128)}, f32[512,256]{1,0:T(8,128)}, u32[]{:S(2)}, u32[]{:S(2)}) %collective-permute-start.7) | collective-permute-done | bytes 524320 | tf_op jit(solution)/shard_map/ppermute | solution.py:605
  76.4 0.4 collective-permute-start.14
  76.9 7.5 %down.1.before = f32[4,512,256]{2,1,0:T(8,128)} custom-call(s32[4,9]{1,0:T(4,128)} %bitcast.23, f32[4,8,512]{2,1,0:T(8,128)} %get-tuple-element.41.place8, bf16[4,36,64,64]{3,2,1,0:T(8,128)(2,1)} %bitcast.12, f32[784,256]{1,0:T(8,128)} %collective-permute-done.8.left_y, f32[784,256]{1,0:T(8,128)} %collective-permute-done.9.right_y, ...), custom_call_target="tpu_custom_call", output_to_operand_aliasing={{}: (7, {})} | custom-call | flops 1000 | bytes 1000 | tf_op jit(solution)/shard_map/down/pallas_call | solution.py:334
  84.4 7.2 %last.1 = f32[4,512,256]{2,1,0:T(8,128)} custom-call(s32[4,9]{1,0:T(4,128)} %bitcast.24, f32[4,8,512]{2,1,0:T(8,128)} %get-tuple-element.41.place8, f32[784,256]{1,0:T(8,128)} %collective-permute-done.3.refs_0_.left.a_left, f32[784,256]{1,0:T(8,128)} %collective-permute-done.4.refs_1_.right.a_right, ...), custom_call_target="tpu_custom_call", output_to_operand_aliasing={{}: (9, {})} | custom-call | flops 20000000000 | bytes 4000000 | tf_op jit(solution)/shard_map/last/pallas_call | solution.py:334
  (12 shorter events, 0.2 us)
Async XLA Ops:
  5.7 14.0 %collective-permute-start = (f32[1296,256]{1,0:T(8,128)}, f32[1296,256]{1,0:T(8,128)}, u32[]{:S(2)}, u32[]{:S(2)}) collective-permute-start(f32[1296,256]{1,0:T(8,128)} %get-tuple-element.36), channel_id=1, source_target_pairs={{0,8},{8,0},{16,24},{24,16},{1,9},{9,1},{17,25},{25,17},{2,10},{10... | collective-permute-start | bytes 3981320 | tf_op jit(solution)/shard_map/ppermute | solution.py:584
  6.5 3.9 %collective-permute-start.1 = (f32[64,256]{1,0:T(8,128)}, f32[64,256]{1,0:T(8,128)S(1)}, u32[]{:S(2)}, u32[]{:S(2)}) collective-permute-start(f32[64,256]{1,0:T(8,128)} %get-tuple-element.37), channel_id=1, source_target_pairs={{0,1},{1,0},{2,3},{3,2},{4,5},{5,4},{6,7},{7,6},{8,9},{9,8},{10,11... | collective-permute-start | bytes 196616 | tf_op jit(solution)/shard_map/ppermute | solution.py:583
  7.7 36.2 %collective-permute-start.3 = (f32[784,256]{1,0:T(8,128)}, f32[784,256]{1,0:T(8,128)}, u32[]{:S(2)}, u32[]{:S(2)}) collective-permute-start(f32[784,256]{1,0:T(8,128)} %get-tuple-element.42.msg.own), channel_id=1, source_target_pairs={{0,1},{1,2},{2,3},{3,4},{4,5},{5,6},{6,7},{7,0},{8,9},{9,10},{10,1... | collective-permute-start | bytes 2408456 | tf_op jit(solution)/shard_map/ppermute | solution.py:588
  8.0 38.0 %collective-permute-start.4 = (f32[784,256]{1,0:T(8,128)}, f32[784,256]{1,0:T(8,128)}, u32[]{:S(2)}, u32[]{:S(2)}) collective-permute-start(f32[784,256]{1,0:T(8,128)} %get-tuple-element.43), channel_id=1, source_target_pairs={{0,7},{1,0},{2,1},{3,2},{4,3},{5,4},{6,5},{7,6},{8,15},{9,8},{10,9... | collective-permute-start | bytes 2408456 | tf_op jit(solution)/shard_map/ppermute | solution.py:589
  11.2 6.5 %collective-permute-start.2 = (f32[128,256]{1,0:T(8,128)S(1)}, f32[128,256]{1,0:T(8,128)S(1)}, u32[]{:S(2)}, u32[]{:S(2)}) collective-permute-start(f32[128,256]{1,0:T(8,128)S(1)} %pad_maximum_fusion), channel_id=1, source_target_pairs={{0,16},{8,24},{16,0},{24,8},{1,17},{9,25},{17,1},{25,9},{2,18},{10... | collective-permute-start | bytes 393224 | tf_op jit(solution)/shard_map/ppermute | solution.py:591
  14.0 19.7 %collective-permute-start.5 = (f32[1296,256]{1,0:T(8,128)}, f32[1296,256]{1,0:T(8,128)}, u32[]{:S(2)}, u32[]{:S(2)}) collective-permute-start(f32[1296,256]{1,0:T(8,128)} %get-tuple-element.46), channel_id=1, source_target_pairs={{8,16},{16,8},{9,17},{17,9},{10,18},{18,10},{11,19},{19,11},{12,20... | collective-permute-start | bytes 3981320 | tf_op jit(solution)/shard_map/ppermute | solution.py:586
  18.4 33.1 %collective-permute-start.10 = (f32[256,256]{1,0:T(8,128)}, f32[256,256]{1,0:T(8,128)}, u32[]{:S(2)}, u32[]{:S(2)}) collective-permute-start(f32[256,256]{1,0:T(8,128)} %constant_dynamic-update-slice_fusion.refs_2_), channel_id=1, source_target_pairs={{0,2},{1,3},{2,4},{3,5},{4,6},{5,7},{6,0},{7,1},{8,10},{9,11},{10,... | collective-permute-start | bytes 786440 | tf_op jit(solution)/shard_map/ppermute | solution.py:595
  19.7 33.0 %collective-permute-start.12 = (f32[256,256]{1,0:T(8,128)}, f32[256,256]{1,0:T(8,128)}, u32[]{:S(2)}, u32[]{:S(2)}) collective-permute-start(f32[256,256]{1,0:T(8,128)} %constant_dynamic-update-slice_fusion.refs_2_), channel_id=1, source_target_pairs={{0,6},{1,7},{2,0},{3,1},{4,2},{5,3},{6,4},{7,5},{8,14},{9,15},{10,... | collective-permute-start | bytes 786440 | tf_op jit(solution)/shard_map/ppermute | solution.py:595
  33.7 20.3 %collective-permute-start.11 = (f32[256,256]{1,0:T(8,128)}, f32[256,256]{1,0:T(8,128)}, u32[]{:S(2)}, u32[]{:S(2)}) collective-permute-start(f32[256,256]{1,0:T(8,128)} %constant_dynamic-update-slice_fusion.refs_2_), channel_id=1, source_target_pairs={{0,4},{1,5},{2,6},{3,7},{4,0},{5,1},{6,2},{7,3},{8,12},{9,13},{10,... | collective-permute-start | bytes 786440 | tf_op jit(solution)/shard_map/ppermute | solution.py:595
  46.0 30.4 %collective-permute-start.8 = (f32[784,256]{1,0:T(8,128)}, f32[784,256]{1,0:T(8,128)}, u32[]{:S(2)}, u32[]{:S(2)}) collective-permute-start(f32[784,256]{1,0:T(8,128)} %collective-permute-done.3.refs_0_.left.a_left), channel_id=1, source_target_pairs={{8,16},{16,8},{9,17},{17,9},{10,18},{18,10},{11,19},{19,11},{12,20... | collective-permute-start | bytes 2408456 | tf_op jit(solution)/shard_map/ppermute | solution.py:606
  49.5 26.9 %collective-permute-start.9 = (f32[784,256]{1,0:T(8,128)}, f32[784,256]{1,0:T(8,128)}, u32[]{:S(2)}, u32[]{:S(2)}) collective-permute-start(f32[784,256]{1,0:T(8,128)} %collective-permute-done.4.refs_1_.right.a_right), channel_id=1, source_target_pairs={{8,16},{16,8},{9,17},{17,9},{10,18},{18,10},{11,19},{19,11},{12,20... | collective-permute-start | bytes 2408456 | tf_op jit(solution)/shard_map/ppermute | solution.py:607
  51.5 22.3 %collective-permute-start.6 = (f32[512,256]{1,0:T(8,128)}, f32[512,256]{1,0:T(8,128)}, u32[]{:S(2)}, u32[]{:S(2)}) collective-permute-start(f32[512,256]{1,0:T(8,128)} %get-tuple-element.53), channel_id=1, source_target_pairs={{0,1},{1,2},{2,3},{3,4},{4,5},{5,6},{6,7},{7,0},{8,9},{9,10},{10,1... | collective-permute-start | bytes 1572872 | tf_op jit(solution)/shard_map/ppermute | solution.py:604
  52.7 23.6 %collective-permute-start.7 = (f32[512,256]{1,0:T(8,128)}, f32[512,256]{1,0:T(8,128)}, u32[]{:S(2)}, u32[]{:S(2)}) collective-permute-start(f32[512,256]{1,0:T(8,128)} %get-tuple-element.54), channel_id=1, source_target_pairs={{0,7},{1,0},{2,1},{3,2},{4,3},{5,4},{6,5},{7,6},{8,15},{9,8},{10,9... | collective-permute-start | bytes 1572872 | tf_op jit(solution)/shard_map/ppermute | solution.py:605
  56.5 6.2 %collective-permute-start.13 = (f32[1568,256]{1,0:T(8,128)}, f32[1568,256]{1,0:T(8,128)}, u32[]{:S(2)}, u32[]{:S(2)}) collective-permute-start(f32[1568,256]{1,0:T(8,128)} %pack.1.devices), channel_id=1, source_target_pairs={{0,8},{8,0},{16,24},{24,16},{1,9},{9,1},{17,25},{25,17},{2,10},{10... | collective-permute-start | bytes 4816904 | tf_op jit(solution)/shard_map/ppermute | solution.py:609
  76.4 8.0 %collective-permute-start.14 = (f32[512,256]{1,0:T(8,128)}, f32[512,256]{1,0:T(8,128)}, u32[]{:S(2)}, u32[]{:S(2)}) collective-permute-start(f32[512,256]{1,0:T(8,128)} %collective-permute-done.6.left), channel_id=1, source_target_pairs={{0,8},{8,0},{16,24},{24,16},{1,9},{9,1},{17,25},{25,17},{2,10},{10... | collective-permute-start | bytes 1572872 | tf_op jit(solution)/shard_map/ppermute | solution.py:634
  76.8 7.6 %collective-permute-start.15 = (f32[512,256]{1,0:T(8,128)}, f32[512,256]{1,0:T(8,128)}, u32[]{:S(2)}, u32[]{:S(2)}) collective-permute-start(f32[512,256]{1,0:T(8,128)} %collective-permute-done.7.right), channel_id=1, source_target_pairs={{0,8},{8,0},{16,24},{24,16},{1,9},{9,1},{17,25},{25,17},{2,10},{10... | collective-permute-start | bytes 1572872 | tf_op jit(solution)/shard_map/ppermute | solution.py:635
